TPU v7x, 32 devices: a whole 2x2x4 slice. The times are simulated.
32 devices in a mesh: groups: 2 (over x), col: 16 (over z, y, core).
Axes of the slice: x: 2, y: 2, z: 4, core: 2. Of those that a mesh axis runs over, the one named last changes fastest.
Arguments:
- field: bfloat16 [3072, 8, 16384], P(('groups', 'col')), parts along dimension 0, may hold values from -6 to 6
- left_first: bfloat16 [16384, 128], replicated, may hold values from -0.046875 to 0.046875
- left_second: bfloat16 [128, 8, 128], replicated, may hold values from -0.1875 to 0.1875
- right_second: bfloat16 [160, 8, 160], replicated, may hold values from -0.15625 to 0.15625
- right_last: bfloat16 [160, 1536], P(None, 'col'), may hold values from -0.15625 to 0.15625
Outputs:
- core_first: float32 [32768, 128], P(('groups', 'col')), parts along dimension 0
- core_middle: float32 [256, 8, 128], P('groups'), parts along dimension 0
- core_last: float32 [3072, 128], P(('groups', 'col')), parts along dimension 0
There are 2 independent parts, one for each index of `groups`. A program takes and returns all parts, laid end to end along the dimension named above; an argument that names none is the same for every part. Nothing has to cross between parts.
All inputs are finite; a program needn't handle non-finite values.
Results may differ from a plain program's by a relative error of at most 0.0098.
Values may be sent and summed in bfloat16 or wider, within the bound.
A program may use at most 128 MiB of HBM per device.

v0:
```python
import jax
import jax.numpy as jnp
from jax import lax
from jax.sharding import PartitionSpec as P


def solve_right(omega):
    gram = jnp.dot(omega, omega.T, precision=lax.Precision.HIGHEST)
    ridge = 0.001 * jnp.trace(gram) / gram.shape[0]
    gram = gram + ridge * jnp.eye(gram.shape[0], dtype=jnp.float32)
    lower = jnp.linalg.cholesky(gram)
    half = lax.linalg.triangular_solve(lower, omega, left_side=True, lower=True)
    return lax.linalg.triangular_solve(lower, half, left_side=True, lower=True, transpose_a=True)


def body(field, left_first, left_second, right_second, right_last):
    high = lax.Precision.HIGHEST
    col_count, steps, cells = field.shape
    rank_left = left_first.shape[1]
    rank_right = right_second.shape[0]
    second_wide = left_second.astype(jnp.float32)
    cross = jnp.einsum(
        "atb,bc->cta", right_second, right_last, preferred_element_type=jnp.float32
    ).astype(jnp.bfloat16)
    flat = field.reshape(col_count * steps, cells)
    psi_local = lax.dot_general(
        flat,
        cross.reshape(col_count * steps, rank_right),
        (((0,), (0,)), ((), ())),
        preferred_element_type=jnp.float32,
    )
    left = jnp.dot(flat, left_first, preferred_element_type=jnp.float32).reshape(
        col_count, steps, rank_left
    )
    middle_term = jnp.einsum("ctr,sc->rts", left, right_last.astype(jnp.float32), precision=high)
    core_last = jnp.einsum("ctr,rtq->cq", left, second_wide, precision=high)
    omega_term = jnp.dot(left_first.astype(jnp.float32).T, psi_local, precision=high)
    psi_middle, omega_first = lax.psum((middle_term, omega_term), "col")
    factor_first = solve_right(omega_first)
    core_first = lax.psum_scatter(
        jnp.dot(psi_local, factor_first.T, precision=high), "col", scatter_dimension=0, tiled=True
    )
    omega_middle = jnp.einsum("rtq,rts->qs", second_wide, psi_middle, precision=high)
    core_middle = jnp.einsum("rts,qs->rtq", psi_middle, solve_right(omega_middle), precision=high)
    return (core_first, core_middle, core_last)


def solution(mesh):
    return jax.shard_map(
        body,
        mesh=mesh,
        in_specs=(P(("groups", "col"), None, None), P(), P(), P(), P(None, "col")),
        out_specs=(P(("groups", "col"), None), P("groups", None, None), P(("groups", "col"), None)),
        check_vma=False,
    )
```

profile of v0, /device:TPU:13, one launch (start us, length us, event | category | flops | bytes accessed | tf_op | source)
XLA Modules:
  0.0 350.0 jit_solution(5969317804030631811)
XLA Ops:
  7.2 0.0 all-reduce.3.cloned.1.call-start
  7.2 12.8 %fusion.5 = f32[96,8,128]{2,1,0:T(8,128)S(1)} fusion(bf16[96,8,16384]{2,1,0:T(8,128)(2,1)} %param.10, bf16[16384,128]{1,0:T(8,128)(2,1)} %param.11), kind=kOutput, calls=%fused_computation.3 | convolution fusion | flops 3221225472 | bytes 29753344 | tf_op jit(solution)/shard_map/dot_general | solution.py:32
  20.1 1.3 convolution_bitcast_fusion
  21.4 56.0 %fusion.2 = f32[160,16384]{1,0:T(8,128)} fusion(bf16[96,8,16384]{2,1,0:T(8,128)(2,1)} %param.10, bf16[160,8,160]{2,1,0:T(8,128)(2,1)S(1)} %copy-done, bf16[160,96]{1,0:T(8,128)(2,1)S(1)} %copy-done.3), kind=kOutput, calls=%fused_computation.2 | convolution fusion | flops 4065976320 | bytes 36091904 | tf_op jit(solution)/shard_map/dot_general | solution.py:26
  77.5 10.5 %convolution_bitcast_fusion.1 = f32[128,160]{0,1:T(8,128)} fusion(f32[160,16384]{1,0:T(8,128)} %fusion.2, bf16[16384,128]{1,0:T(8,128)(2,1)} %param.11), kind=kOutput, calls=%fused_computation.8 | convolution fusion | flops 4026531840 | bytes 14761984 | tf_op jit(solution)/shard_map/dot_general | solution.py:37
  87.9 0.0 all-reduce.3.cloned.1.call-update
  88.0 0.0 reduce-scatter.2.cloned.1.call-start
  88.0 91.3 %all-reduce.3.cloned.1.call-done = (f32[128,160]{0,1:T(8,128)}, f32[128,8,160]{0,2,1:T(8,128)}) async-done(((f32[128,160]{0,1:T(8,128)}, f32[128,8,160]{0,2,1:T(8,128)}), (f32[128,160]{0,1:T(8,128)}, f32[128,8,160]{0,2,1:T(8,128)})) %all-reduce.3.cloned.1.call-update) | async-done | bytes 737296 | tf_op jit(solution)/shard_map/psum | solution.py:38
  179.3 2.0 select_reduce_fusion.3
  182.0 0.1 copy.11
  182.1 11.7 %cholesky.44 = f32[128,128]{1,0:T(8,128)S(1)} custom-call(f32[128,128]{1,0:T(8,128)S(1)} %fusion.26), custom_call_target="Cholesky" | custom-call | tf_op jit(solution)/shard_map/jit(cholesky)/cholesky | solution.py:11
  193.8 0.6 compare_reduce_fusion.1
  194.5 0.7 fusion.17
  195.2 9.8 %custom-call.11 = f32[1,128,128]{1,2,0:T(8,128)S(1)} custom-call(f32[1,128,128]{2,1,0:T(8,128)S(1)} %fusion.17), custom_call_target="InvertDiagBlocksLowerTriangular" | custom-call | tf_op jit(solution)/shard_map/triangular_solve/custom-call.2 | solution.py:13
  205.0 1.2 fusion.22
  206.2 0.3 fusion.24
  206.5 30.3 %fusion.30 = f32[16384,128]{1,0:T(8,128)} fusion(f32[160,16384]{1,0:T(8,128)} %fusion.2, f32[128,160]{1,0:T(8,128)S(1)} %fusion.24), kind=kOutput, calls=%fused_computation.46 | convolution fusion | flops 4026531840 | bytes 18956288 | tf_op jit(solution)/shard_map/dot_general | solution.py:41
  236.8 0.0 reduce-scatter.2.cloned.1.call-update
  236.8 0.3 copy.25
  237.1 1.2 convolution_bitcast_fusion.3
  238.3 0.5 copy.23
  238.8 0.4 fusion.11
  239.2 1.0 select_reduce_fusion.2
  240.9 0.1 copy.16
  241.1 11.7 %cholesky.55 = f32[128,128]{1,0:T(8,128)S(1)} custom-call(f32[128,128]{1,0:T(8,128)S(1)} %fusion.21), custom_call_target="Cholesky" | custom-call | tf_op jit(solution)/shard_map/jit(cholesky)/cholesky | solution.py:11
  252.8 0.6 compare_reduce_fusion
  253.4 0.7 fusion.18
  254.1 9.8 %custom-call.13 = f32[1,128,128]{1,2,0:T(8,128)S(1)} custom-call(f32[1,128,128]{2,1,0:T(8,128)S(1)} %fusion.18), custom_call_target="InvertDiagBlocksLowerTriangular" | custom-call | tf_op jit(solution)/shard_map/triangular_solve/custom-call.2 | solution.py:13
  263.9 0.3 fusion.13
  264.3 0.4 convolution_bitcast_fusion.2
  264.6 1.8 fusion.31
  266.4 76.6 %reduce-scatter.2.cloned.1.call-done = f32[1024,128]{1,0:T(8,128)} async-done(((f32[16384,128]{1,0:T(8,128)}), f32[1024,128]{1,0:T(8,128)}) %reduce-scatter.2.cloned.1.call-update) | async-done | bytes 524304 | tf_op jit(solution)/shard_map/reduce_scatter | solution.py:40
  (14 shorter events, 0.2 us)
Async XLA Ops:
  7.2 14.3 %copy-start = (bf16[160,8,160]{2,1,0:T(8,128)(2,1)S(1)}, bf16[160,8,160]{2,1,0:T(8,128)(2,1)}, u32[]{:S(2)}) copy-start(bf16[160,8,160]{2,1,0:T(8,128)(2,1)} %param.13) | copy-start | bytes 1228804
  7.2 12.9 %copy-start.3 = (bf16[160,96]{1,0:T(8,128)(2,1)S(1)}, bf16[160,96]{1,0:T(8,128)(2,1)}, u32[]{:S(2)}) copy-start(bf16[160,96]{1,0:T(8,128)(2,1)} %param.14) | copy-start | bytes 92164
  7.2 172.1 %all-reduce.3.cloned.1.call-start = ((), (), s32[]{:S(2)}) async-start(), calls=%async_computation.2 | async-start | bytes 1474560 | tf_op jit(solution)/shard_map/psum | solution.py:38
  88.0 255.0 %reduce-scatter.2.cloned.1.call-start = ((), (), s32[]{:S(2)}) async-start(), calls=%async_computation.1 | async-start | bytes 8912896 | tf_op jit(solution)/shard_map/reduce_scatter | solution.py:40
  206.5 30.6 %copy-start.2 = (bf16[128,8,128]{2,1,0:T(8,128)(2,1)S(1)}, bf16[128,8,128]{2,1,0:T(8,128)(2,1)}, u32[]{:S(2)}) copy-start(bf16[128,8,128]{2,1,0:T(8,128)(2,1)} %param.12) | copy-start | bytes 786436
  236.8 1.5 copy-start.1
Sparse Core Ops, SparseCore 0:
  88.1 91.1 all-reduce.2
  236.9 106.0 reduce-scatter.1
where the time goes:
time: 355 us; the launch traced here: 350 us
  waiting for transfers between devices  168 us (47%)
  matrix products  120 us (34%)
  other arithmetic  45.8 us (13%)
  between operations  15.8 us (4%)
    psum x1, waiting for transfers between devices, body(): psi_middle, omega_first = lax.psum((middle_term, omega_term), 'col')  91.3 us
    reduce_scatter x1, waiting for transfers between devices, body(): lax.psum_scatter(jnp.dot(psi_local, factor_first.T, precision=high), 'col...  76.6 us
    dot_general x1, matrix products, body(): lax.dot_general(flat, cross.reshape(col_count * steps, rank_right), (((0,...  56 us
    dot_general x1, matrix products, body(): jnp.dot(psi_local, factor_first.T, precision=high)  30.3 us
    another operation x6, other arithmetic, solve_right(): lower = jnp.linalg.cholesky(gram)  24.8 us
    another operation x4, other arithmetic, solve_right(): lax.linalg.triangular_solve(lower, half, left_side=True, lower=True, tran...  20.9 us
    dot_general x1, matrix products, body(): jnp.dot(flat, left_first, preferred_element_type=jnp.float32)  12.8 us
    dot_general x1, matrix products, body(): jnp.dot(left_first.astype(jnp.float32).T, psi_local, precision=high)  10.5 us
  transfers between devices with their start and end apart: 2, of which 2 were waited for; matrix products, arithmetic and copies ran while one was open for 8% of the time, Pallas kernels for 0%

commit v1 on v0

v1 whole, which is shorter than its diff:
```python
import functools

import jax
import jax.numpy as jnp
from jax import lax
from jax.experimental import pallas as pl
from jax.experimental.pallas import tpu as pltpu
from jax.sharding import PartitionSpec as P

HIGH = lax.Precision.HIGHEST
MESH = pl.DeviceIdType.MESH


def solve_right(omega):
    gram = jnp.dot(omega, omega.T, precision=HIGH)
    ridge = 0.001 * jnp.trace(gram) / gram.shape[0]
    gram = gram + ridge * jnp.eye(gram.shape[0], dtype=jnp.float32)
    lower = jnp.linalg.cholesky(gram)
    half = lax.linalg.triangular_solve(lower, omega, left_side=True, lower=True)
    return lax.linalg.triangular_solve(lower, half, left_side=True, lower=True, transpose_a=True)


def remote(src, dst, send_sem, recv_sem, target):
    return pltpu.make_async_remote_copy(
        src_ref=src, dst_ref=dst, send_sem=send_sem, recv_sem=recv_sem,
        device_id={"col": target}, device_id_type=MESH,
    )


def sketch_kernel(
    n, cross_ref, field_ref, wide_ref, half_ref, psi_ref, wide_out, half_out,
    chunk, a_send, a_recv, a_keep, b_send, b_recv, b_keep, c_send, c_recv,
    w_recv, h_recv, w_all, h_all,
    load_sem, a_ss, a_rs, b_ss, b_rs, c_ss, c_rs, w_ss, w_rs, h_ss, h_rs, w2_ss, w2_rs, h2_ss, h2_rs,
):
    far = n // 4
    me = lax.axis_index("col")
    core = lax.rem(me, 2)
    y = lax.rem(me // 2, 2)
    z = me // 4
    block = psi_ref.shape[1]
    span = 4 * block

    def goal(k):
        return lax.rem(z + 1 + k, far)

    def load(k):
        start = pl.multiple_of(goal(k) * span, span)
        return pltpu.make_async_copy(field_ref.at[:, pl.ds(start, span)], chunk.at[k % 2], load_sem.at[k % 2])

    load(0).start()
    barrier = pltpu.get_barrier_semaphore()

    @pl.loop(1, n)
    def _(j):
        pl.semaphore_signal(barrier, inc=1, device_id={"col": lax.rem(me + j, n)}, device_id_type=MESH)

    pl.semaphore_wait(barrier, n - 1)

    def spread_wide(j):
        to = lax.rem(me + j, n)
        return remote(wide_ref.at[to], w_recv.at[j], w_ss.at[j], w_rs.at[j], to)

    def spread_half(j):
        to = lax.rem(me + j, n)
        return remote(half_ref.at[to], h_recv.at[j], h_ss.at[j], h_rs.at[j], to)

    def share_wide(j):
        return remote(w_all.at[0], w_all.at[j], w2_ss.at[j], w2_rs.at[j], lax.rem(me + j, n))

    def share_half(j):
        return remote(h_all.at[0], h_all.at[j], h2_ss.at[j], h2_rs.at[j], lax.rem(me + j, n))

    @pl.loop(1, n)
    def _(j):
        spread_wide(j).start()
        spread_half(j).start()

    def copy_a(k):
        return remote(a_send.at[k], a_recv.at[k], a_ss.at[k], a_rs.at[k], me + 1 - 2 * core)

    def copy_b(k):
        return remote(b_send.at[k], b_recv.at[k], b_ss.at[k], b_rs.at[k], me + 2 - 4 * y)

    def copy_c(k):
        return remote(c_send.at[k], c_recv.at[k], c_ss.at[k], c_rs.at[k], (goal(k) * 2 + y) * 2 + core)

    def product(k, row, which):
        start = pl.multiple_of((row * 2 + which) * block, block)
        return jnp.dot(cross_ref[...], chunk[k % 2, :, pl.ds(start, block)], preferred_element_type=jnp.float32)

    def compute(k):
        if k + 1 < far:
            load(k + 1).start()
        load(k).wait()
        for row in range(2):
            a_send[k, row] = product(k, row, 1 - core).astype(jnp.bfloat16)
        copy_a(k).start()
        for row in range(2):
            a_keep[k, row] = product(k, row, core)

    def stage_b(k):
        copy_a(k).wait()
        b_send[k] = (a_keep[k, 1 - y] + a_recv[k, 1 - y].astype(jnp.float32)).astype(jnp.bfloat16)
        copy_b(k).start()
        b_keep[k] = a_keep[k, y] + a_recv[k, y].astype(jnp.float32)

    def stage_c(k):
        copy_b(k).wait()
        total = b_keep[k] + b_recv[k].astype(jnp.float32)
        if k < far - 1:
            c_send[k] = total.astype(jnp.bfloat16)
            copy_c(k).start()
        else:
            psi_ref[...] = total

    for k in range(far + 2):
        if k < far:
            compute(k)
        if 1 <= k <= far:
            stage_b(k - 1)
        if k == min(1, far - 1):

            @pl.loop(1, n)
            def _(j):
                spread_wide(j).wait()
                spread_half(j).wait()

            w_all[0] = lax.fori_loop(1, n, lambda j, s: s + w_recv[j], wide_ref[me])
            h_all[0] = lax.fori_loop(
                1, n, lambda j, s: s + h_recv[j].astype(jnp.float32), half_ref[me].astype(jnp.float32)
            ).astype(jnp.bfloat16)

            @pl.loop(1, n)
            def _(j):
                share_wide(j).start()
                share_half(j).start()

        if k >= 2:
            stage_c(k - 2)

    @pl.loop(1, n)
    def _(j):
        share_wide(j).wait()
        share_half(j).wait()

    wide_out[me] = w_all[0]
    half_out[me] = h_all[0]

    @pl.loop(1, n)
    def _(j):
        source = lax.rem(me - j + n, n)
        wide_out[source] = w_all[j]
        half_out[source] = h_all[j]

    for k in range(far - 1):
        copy_c(k).wait()
        psi_ref[...] += c_recv[k].astype(jnp.float32)


def sketch(n, cross, flat, wide, half):
    rank, depth = cross.shape
    cells = flat.shape[1]
    block, far = cells // n, n // 4
    low, full = jnp.bfloat16, jnp.float32
    dma = pltpu.SemaphoreType.DMA
    vmem = pl.BlockSpec(memory_space=pltpu.VMEM)
    return pl.pallas_call(
        functools.partial(sketch_kernel, n),
        out_shape=(
            jax.ShapeDtypeStruct((rank, block), full),
            jax.ShapeDtypeStruct(wide.shape, full),
            jax.ShapeDtypeStruct(half.shape, low),
        ),
        in_specs=[vmem, pl.BlockSpec(memory_space=pl.ANY), vmem, vmem],
        out_specs=(vmem, vmem, vmem),
        scratch_shapes=[
            pltpu.VMEM((2, depth, 4 * block), low),
            pltpu.VMEM((far, 2, rank, block), low),
            pltpu.VMEM((far, 2, rank, block), low),
            pltpu.VMEM((far, 2, rank, block), full),
            pltpu.VMEM((far, rank, block), low),
            pltpu.VMEM((far, rank, block), low),
            pltpu.VMEM((far, rank, block), full),
            pltpu.VMEM((far, rank, block), low),
            pltpu.VMEM((far, rank, block), low),
            pltpu.VMEM(wide.shape, full),
            pltpu.VMEM(half.shape, low),
            pltpu.VMEM(wide.shape, full),
            pltpu.VMEM(half.shape, low),
            dma((2,)),
            *[dma((far,)) for _ in range(6)],
            *[dma((n,)) for _ in range(8)],
        ],
        compiler_params=pltpu.CompilerParams(
            collective_id=0, has_side_effects=True, vmem_limit_bytes=56 * 2**20
        ),
        cost_estimate=pl.CostEstimate(
            flops=2 * rank * depth * cells, bytes_accessed=2 * depth * cells, transcendentals=0
        ),
    )(cross, flat, wide, half)


def split_rows(x, n, tile):
    rows = -(-x.size // (n * 128))
    rows = -(-rows // tile) * tile
    x = jnp.pad(x.reshape(-1), (0, n * rows * 128 - x.size))
    return x.reshape(n, rows, 128)


def body(n, field, left_first, left_second, right_second, right_last):
    col_count, steps, cells = field.shape
    rank_left = left_first.shape[1]
    rank_right = right_second.shape[0]
    flat = field.reshape(col_count * steps, cells)
    cross = jnp.einsum(
        "atb,bc->act", right_second, right_last, preferred_element_type=jnp.float32
    ).astype(jnp.bfloat16).reshape(rank_right, col_count * steps)
    left = jnp.dot(flat, left_first, preferred_element_type=jnp.float32)
    left_wide = left.reshape(col_count, steps, rank_left)
    last_wide = right_last.astype(jnp.float32)
    middle_term = jnp.einsum("ctr,sc->rts", left_wide, last_wide, precision=HIGH)
    core_last = jnp.einsum("ctr,rtq->cq", left_wide, left_second.astype(jnp.float32), precision=HIGH)
    omega_first_term = jnp.einsum("kr,ak->ra", left, cross.astype(jnp.float32), precision=HIGH)
    omega_middle_term = jnp.einsum("cq,ac->qa", core_last, last_wide, precision=HIGH)
    omega_term = jnp.stack([omega_first_term, omega_middle_term])
    psi, wide, half = sketch(
        n, cross, flat, split_rows(omega_term, n, 8), split_rows(middle_term.astype(jnp.bfloat16), n, 16)
    )
    omega = wide.reshape(-1)[: omega_term.size].reshape(omega_term.shape)
    psi_middle = half.reshape(-1)[: middle_term.size].reshape(middle_term.shape).astype(jnp.float32)
    core_first = jnp.einsum("ag,ra->gr", psi, solve_right(omega[0]), precision=HIGH)
    core_middle = jnp.einsum("rts,qs->rtq", psi_middle, solve_right(omega[1]), precision=HIGH)
    return (core_first, core_middle, core_last)


def solution(mesh):
    return jax.shard_map(
        functools.partial(body, mesh.shape["col"]),
        mesh=mesh,
        in_specs=(P(("groups", "col"), None, None), P(), P(), P(), P(None, "col")),
        out_specs=(P(("groups", "col"), None), P("groups", None, None), P(("groups", "col"), None)),
        check_vma=False,
    )
```

time: 355 us -> 142 us (0.40); the launches traced: 350 us -> 141 us
  waiting for transfers between devices: 168 us -> 0 us
  matrix products: 120 us -> 23.7 us
  Pallas kernels: 0 us -> 60.8 us
  between operations: 15.8 us -> 2.22 us
  local copies, waits for them, and re-layouts: 0.94 us -> 8.35 us
    dot_general x10, matrix products: 117 us -> 22.5 us  [the longest x1 12.8 us: body(): left = jnp.dot(flat, left_first, preferred_element_type=jnp.float32)]
    psum x1 -> x0, waiting for transfers between devices: 91.3 us -> none  [body(): psi_middle, omega_first = lax.psum((middle_term, omega_term), 'col')]
    reduce_scatter x1 -> x0, waiting for transfers between devices: 76.6 us -> none  [body(): lax.psum_scatter(jnp.dot(psi_local, factor_first.T, precision=high), 'col...]
    pallas_call x0 -> x1, Pallas kernels: none -> 60.8 us  [sketch(): pl.pallas_call(functools.partial(sketch_kernel, n), out_shape=(jax.ShapeD...]
  transfers between devices with their start and end apart: 2 -> 0, of which waited for: 2 -> 0; matrix products, arithmetic and copies ran while one was open for 8% -> 0% of each run, Pallas kernels for 0% -> 0%
where the time goes in v1:
time: 142 us; the launch traced here: 141 us
  Pallas kernels  60.8 us (43%)
  other arithmetic  46 us (32%)
  matrix products  23.7 us (17%)
  local copies, waits for them, and re-layouts  8.35 us (6%)
  between operations  2.22 us (2%)
    pallas_call x1, Pallas kernels, sketch(): pl.pallas_call(functools.partial(sketch_kernel, n), out_shape=(jax.ShapeD...  60.8 us
    another operation x6, other arithmetic, solve_right(): lower = jnp.linalg.cholesky(gram)  24.8 us
    another operation x4, other arithmetic, solve_right(): lax.linalg.triangular_solve(lower, half, left_side=True, lower=True, tran...  21.1 us
    dot_general x1, matrix products, body(): left = jnp.dot(flat, left_first, preferred_element_type=jnp.float32)  12.8 us
    dot_general x1, matrix products, body(): jnp.einsum('ag,ra->gr', psi, solve_right(omega[0]), precision=HIGH)  3.73 us

profile of v1, /device:TPU:13, one launch (start us, length us, event | category | flops | bytes accessed | tf_op | source)
XLA Modules:
  0.0 141.0 jit_solution(12417233780072530044)
XLA Ops:
  0.7 1.1 copy-done
  1.7 1.1 fusion
  2.8 0.3 copy.23
  3.2 0.8 copy.29.cross_ref
  4.0 12.8 %fusion.17 = f32[768,128]{1,0:T(8,128)S(1)} fusion(bf16[16384,128]{1,0:T(8,128)(2,1)} %param.11, bf16[96,8,16384]{2,1,0:T(8,128)(2,1)} %param.10), kind=kOutput, calls=%fused_computation.39 | convolution fusion | flops 3221225472 | bytes 29753344 | tf_op jit(solution)/shard_map/dot_general | solution.py:219
  16.8 0.5 convolution_bitcast_fusion.2
  17.3 0.5 fusion.1
  17.8 0.3 copy.38
  18.1 0.6 convolution_bitcast_fusion.3
  19.0 0.2 reshape.54
  19.2 0.7 pad.4
  19.9 0.4 copy.28
  20.3 1.6 %reshape.56.half_ref = bf16[16,80,128]{2,1,0:T(8,128)(2,1)} reshape(bf16[128,8,160]{2,1,0:T(8,128)(2,1)S(1)} %copy.28) | data formatting | bytes 655360 | tf_op jit(solution)/shard_map/reshape | solution.py:208
  21.9 60.8 %shard_map.76 = (f32[160,1024]{1,0:T(8,128)}, f32[16,24,128]{2,1,0:T(8,128)}, bf16[16,80,128]{2,1,0:T(8,128)(2,1)}) custom-call(bf16[160,768]{1,0:T(8,128)(2,1)} %copy.29.cross_ref, bf16[768,16384]{1,0:T(8,128)(2,1)} %bitcast.70, f32[16,24,128]{2,1,0:T(8,128)} %bitcast.74, bf16[16,80,128]{2,1,0:T(8,128)(2,1)} %reshape.56.half_ref), custom_call_target="tpu_custom_call" | custom-call | flops 4026531840 | bytes 25165824 | tf_op jit(solution)/shard_map/pallas_call | solution.py:168
  82.7 0.9 fusion.20
  83.7 0.9 select_reduce_fusion.2
  85.4 11.7 %cholesky.55 = f32[128,128]{1,0:T(8,128)S(1)} custom-call(f32[128,128]{1,0:T(8,128)S(1)} %fusion.9), custom_call_target="Cholesky" | custom-call | tf_op jit(solution)/shard_map/jit(cholesky)/cholesky | solution.py:18
  97.2 0.6 compare_reduce_fusion
  97.8 0.7 fusion.5
  98.5 9.8 %custom-call.13 = f32[1,128,128]{1,2,0:T(8,128)S(1)} custom-call(f32[1,128,128]{2,1,0:T(8,128)S(1)} %fusion.5), custom_call_target="InvertDiagBlocksLowerTriangular" | custom-call | tf_op jit(solution)/shard_map/triangular_solve/custom-call.2 | solution.py:20
  108.3 0.3 fusion.6
  108.6 0.4 convolution_bitcast_fusion
  109.1 0.9 select_reduce_fusion.3
  110.8 11.7 %cholesky.44 = f32[128,128]{1,0:T(8,128)S(1)} custom-call(f32[128,128]{1,0:T(8,128)S(1)} %fusion.14), custom_call_target="Cholesky" | custom-call | tf_op jit(solution)/shard_map/jit(cholesky)/cholesky | solution.py:18
  122.5 0.6 compare_reduce_fusion.1
  123.2 0.7 fusion.4
  123.8 10.0 %custom-call.11 = f32[1,128,128]{1,2,0:T(8,128)S(1)} custom-call(f32[1,128,128]{2,1,0:T(8,128)S(1)} %fusion.4), custom_call_target="InvertDiagBlocksLowerTriangular" | custom-call | tf_op jit(solution)/shard_map/triangular_solve/custom-call.2 | solution.py:20
  133.8 0.3 fusion.10
  134.1 0.3 fusion.12
  134.4 3.7 %fusion.21 = f32[1024,128]{1,0:T(8,128)} fusion(f32[160,1024]{1,0:T(8,128)} %get-tuple-element.9, f32[128,160]{1,0:T(8,128)S(1)} %fusion.12), kind=kOutput, calls=%fused_computation.43 | convolution fusion | flops 251658240 | bytes 1261568 | tf_op jit(solution)/shard_map/ag,ra->gr/dot_general | solution.py:232
  138.1 1.5 %reshape_reshape.3 = bf16[128,8,160]{2,1,0:T(8,128)(2,1)S(1)} reshape(bf16[16,80,128]{2,1,0:T(8,128)(2,1)} %get-tuple-element.11) | data formatting | bytes 655360 | tf_op jit(solution)/shard_map/reshape;reshape | solution.py:231
  139.6 1.4 fusion.22
  (20 shorter events, 0.9 us)
Async XLA Ops:
  0.6 1.1 copy-start
  0.6 16.6 %copy-start.1 = (bf16[160,96]{1,0:T(8,128)(2,1)S(1)}, bf16[160,96]{1,0:T(8,128)(2,1)}, u32[]{:S(2)}) copy-start(bf16[160,96]{1,0:T(8,128)(2,1)} %param.14) | copy-start | bytes 92164
  0.7 17.4 %copy-start.3 = (bf16[128,8,128]{2,1,0:T(8,128)(2,1)S(1)}, bf16[128,8,128]{2,1,0:T(8,128)(2,1)}, u32[]{:S(2)}) copy-start(bf16[128,8,128]{2,1,0:T(8,128)(2,1)} %param.12) | copy-start | bytes 786436
  18.6 122.4 %copy-start.2 = (f32[96,128]{1,0:T(8,128)}, f32[96,128]{1,0:T(8,128)S(1)}, u32[]{:S(2)}) copy-start(f32[96,128]{1,0:T(8,128)S(1)} %convolution_bitcast_fusion.3) | copy-start | bytes 147460

commit v2 on v1

--- a/solution.py
+++ b/solution.py
@@ -11,13 +11,41 @@
 MESH = pl.DeviceIdType.MESH
 
 
-def solve_right(omega):
-    gram = jnp.dot(omega, omega.T, precision=HIGH)
-    ridge = 0.001 * jnp.trace(gram) / gram.shape[0]
-    gram = gram + ridge * jnp.eye(gram.shape[0], dtype=jnp.float32)
-    lower = jnp.linalg.cholesky(gram)
-    half = lax.linalg.triangular_solve(lower, omega, left_side=True, lower=True)
-    return lax.linalg.triangular_solve(lower, half, left_side=True, lower=True, transpose_a=True)
+def ridged_gram(omega):
+    gram = lax.dot_general(
+        omega, omega, (((1,), (1,)), ((), ())), precision=HIGH, preferred_element_type=jnp.float32
+    )
+    rank = gram.shape[0]
+    eye = lax.broadcasted_iota(jnp.int32, gram.shape, 0) == lax.broadcasted_iota(jnp.int32, gram.shape, 1)
+    trace = jnp.sum(jnp.where(eye, gram, 0.0))
+    return gram + jnp.where(eye, 0.001 * trace / rank, 0.0)
+
+
+def eliminate(gram, k):
+    rank = gram.shape[0]
+    at_k = lax.broadcasted_iota(jnp.int32, (1, rank), 1) == k
+    column = jnp.broadcast_to(gram[:, k : k + 1], gram.shape)
+    row = jnp.where(at_k, 1.0, gram[k : k + 1, :]) / column[k : k + 1, :]
+    result = jnp.where(at_k, 0.0, gram) - column * row
+    rows = lax.broadcasted_iota(jnp.int32, (8, rank), 0)
+    head = jnp.where(rows == k, row, result[:8])
+    return jnp.concatenate([head, result[8:]], axis=0)
+
+
+def solve_pair(first, second):
+    rank = first.shape[0]
+
+    def eight(_, pair):
+        for k in range(8):
+            pair = tuple(eliminate(gram, k) for gram in pair)
+        pair = tuple(jnp.concatenate([gram[8:], gram[:8]], axis=0) for gram in pair)
+        return tuple(pltpu.roll(gram, rank - 8, 1) for gram in pair)
+
+    pair = lax.fori_loop(0, rank // 8, eight, (ridged_gram(first), ridged_gram(second)))
+    return [
+        jnp.dot(inverse, omega, precision=HIGH, preferred_element_type=jnp.float32)
+        for inverse, omega in zip(pair, (first, second))
+    ]
 
 
 def remote(src, dst, send_sem, recv_sem, target):
@@ -28,9 +56,9 @@
 
 
 def sketch_kernel(
-    n, cross_ref, field_ref, wide_ref, half_ref, psi_ref, wide_out, half_out,
+    n, rows, cross_ref, field_ref, wide_ref, half_ref, psi_ref, factor_out, half_out,
     chunk, a_send, a_recv, a_keep, b_send, b_recv, b_keep, c_send, c_recv,
-    w_recv, h_recv, w_all, h_all,
+    w_recv, h_recv, w_all, h_all, omega_ref,
     load_sem, a_ss, a_rs, b_ss, b_rs, c_ss, c_rs, w_ss, w_rs, h_ss, h_rs, w2_ss, w2_rs, h2_ss, h2_rs,
 ):
     far = n // 4
@@ -114,6 +142,31 @@
         else:
             psi_ref[...] = total
 
+    def solve():
+        @pl.loop(1, n)
+        def _(j):
+            share_wide(j).wait()
+            share_half(j).wait()
+
+        omega_ref[me] = w_all[0]
+        half_out[me] = h_all[0]
+
+        @pl.loop(1, n)
+        def _(j):
+            source = lax.rem(me - j + n, n)
+            omega_ref[source] = w_all[j]
+            half_out[source] = h_all[j]
+
+        held = omega_ref.shape[1]
+        omega = omega_ref[...].reshape(n * held, omega_ref.shape[2])
+        if held != rows:
+            to = lax.broadcasted_iota(jnp.int32, (n * rows, n * held), 0)
+            at = lax.broadcasted_iota(jnp.int32, (n * rows, n * held), 1)
+            chosen = (to == (at // held) * rows + at % held) & (at % held < rows)
+            omega = jnp.dot(chosen.astype(jnp.float32), omega, precision=HIGH, preferred_element_type=jnp.float32)
+        rank = n * rows // 2
+        factor_out[0], factor_out[1] = solve_pair(omega[:rank], omega[rank:])
+
     for k in range(far + 2):
         if k < far:
             compute(k)
@@ -136,29 +189,17 @@
                 share_wide(j).start()
                 share_half(j).start()
 
+        if k == far + 1:
+            solve()
         if k >= 2:
             stage_c(k - 2)
-
-    @pl.loop(1, n)
-    def _(j):
-        share_wide(j).wait()
-        share_half(j).wait()
-
-    wide_out[me] = w_all[0]
-    half_out[me] = h_all[0]
-
-    @pl.loop(1, n)
-    def _(j):
-        source = lax.rem(me - j + n, n)
-        wide_out[source] = w_all[j]
-        half_out[source] = h_all[j]
 
     for k in range(far - 1):
         copy_c(k).wait()
         psi_ref[...] += c_recv[k].astype(jnp.float32)
 
 
-def sketch(n, cross, flat, wide, half):
+def sketch(n, rows, cross, flat, wide, half):
     rank, depth = cross.shape
     cells = flat.shape[1]
     block, far = cells // n, n // 4
@@ -166,10 +207,10 @@
     dma = pltpu.SemaphoreType.DMA
     vmem = pl.BlockSpec(memory_space=pltpu.VMEM)
     return pl.pallas_call(
-        functools.partial(sketch_kernel, n),
+        functools.partial(sketch_kernel, n, rows),
         out_shape=(
             jax.ShapeDtypeStruct((rank, block), full),
-            jax.ShapeDtypeStruct(wide.shape, full),
+            jax.ShapeDtypeStruct((2, n * rows // 2, rank), full),
             jax.ShapeDtypeStruct(half.shape, low),
         ),
         in_specs=[vmem, pl.BlockSpec(memory_space=pl.ANY), vmem, vmem],
@@ -188,6 +229,7 @@
             pltpu.VMEM(half.shape, low),
             pltpu.VMEM(wide.shape, full),
             pltpu.VMEM(half.shape, low),
+            pltpu.VMEM(wide.shape, full),
             dma((2,)),
             *[dma((far,)) for _ in range(6)],
             *[dma((n,)) for _ in range(8)],
@@ -224,13 +266,15 @@
     omega_first_term = jnp.einsum("kr,ak->ra", left, cross.astype(jnp.float32), precision=HIGH)
     omega_middle_term = jnp.einsum("cq,ac->qa", core_last, last_wide, precision=HIGH)
     omega_term = jnp.stack([omega_first_term, omega_middle_term])
-    psi, wide, half = sketch(
-        n, cross, flat, split_rows(omega_term, n, 8), split_rows(middle_term.astype(jnp.bfloat16), n, 16)
-    )
-    omega = wide.reshape(-1)[: omega_term.size].reshape(omega_term.shape)
+    rows = 2 * rank_left // n
+    held = -(-rows // 8) * 8
+    omega_term = jnp.pad(omega_term.reshape(n, rows, rank_right), ((0, 0), (0, held - rows), (0, 0)))
+    psi, factor, half = sketch(
+        n, rows, cross, flat, omega_term, split_rows(middle_term.astype(jnp.bfloat16), n, 16)
+    )
     psi_middle = half.reshape(-1)[: middle_term.size].reshape(middle_term.shape).astype(jnp.float32)
-    core_first = jnp.einsum("ag,ra->gr", psi, solve_right(omega[0]), precision=HIGH)
-    core_middle = jnp.einsum("rts,qs->rtq", psi_middle, solve_right(omega[1]), precision=HIGH)
+    core_first = jnp.einsum("ag,ra->gr", psi, factor[0], precision=HIGH)
+    core_middle = jnp.einsum("rts,qs->rtq", psi_middle, factor[1], precision=HIGH)
     return (core_first, core_middle, core_last)
 
 

time: 142 us -> 93.7 us (0.66)
  other arithmetic: 46 us -> 0.02 us
  Pallas kernels: 60.8 us -> 63.9 us
  matrix products: 23.7 us -> 21.6 us
  local copies, waits for them, and re-layouts: 8.35 us -> 6.87 us
  between operations: 2.22 us -> 0.77 us
    another operation x10 -> x0, other arithmetic: 45.9 us -> none  [the longest x6 24.8 us: solve_right(): lower = jnp.linalg.cholesky(gram)]
    pallas_call x1, Pallas kernels: 60.8 us -> 63.9 us  [sketch(): pl.pallas_call(functools.partial(sketch_kernel, n, rows), out_shape=(jax....]
    dot_general x4 -> x2, matrix products: 6.87 us -> 6.04 us  [the longest x1 3.74 us: body(): core_first = jnp.einsum('ag,ra->gr', psi, factor[0], precision=HIGH)]
where the time goes in v2:
time: 93.7 us; the launch traced here: 93.2 us
  Pallas kernels  63.9 us (68%)
  matrix products  21.6 us (23%)
  local copies, waits for them, and re-layouts  6.87 us (7%)
    pallas_call x1, Pallas kernels, sketch(): pl.pallas_call(functools.partial(sketch_kernel, n, rows), out_shape=(jax....  63.9 us
    dot_general x1, matrix products, body(): left = jnp.dot(flat, left_first, preferred_element_type=jnp.float32)  12.8 us
    dot_general x1, matrix products, body(): core_first = jnp.einsum('ag,ra->gr', psi, factor[0], precision=HIGH)  3.74 us
    dot_general x1, matrix products, body(): jnp.einsum('rts,qs->rtq', psi_middle, factor[1], precision=HIGH)  2.3 us

profile of v2, /device:TPU:13, one launch (start us, length us, event | category | flops | bytes accessed | tf_op | source)
XLA Modules:
  0.0 93.2 jit_solution(3980214335499214669)
XLA Ops:
  0.6 0.0 copy-start
  0.6 0.0 copy-start.1
  0.7 0.0 copy-start.3
  0.7 1.1 %copy-done = bf16[160,8,160]{2,1,0:T(8,128)(2,1)S(1)} copy-done((bf16[160,8,160]{2,1,0:T(8,128)(2,1)S(1)}, bf16[160,8,160]{2,1,0:T(8,128)(2,1)}, u32[]{:S(2)}) %copy-start) | copy-done | bytes 409624
  1.7 1.1 %fusion = bf16[160,96,8]{1,0,2:T(8,128)(2,1)S(1)} fusion(bf16[160,8,160]{2,1,0:T(8,128)(2,1)S(1)} %copy-done, bf16[160,96]{1,0:T(8,128)(2,1)} %param.9), kind=kOutput, calls=%fused_computation.2 | convolution fusion | flops 39444480 | bytes 686080 | tf_op jit(solution)/shard_map/atb,bc->act/dot_general | solution.py:258
  2.8 0.3 copy.19
  3.2 0.9 copy.25.cross_ref
  4.0 12.8 %fusion.12 = f32[768,128]{1,0:T(8,128)S(1)} fusion(bf16[16384,128]{1,0:T(8,128)(2,1)} %param.6, bf16[96,8,16384]{2,1,0:T(8,128)(2,1)} %param.5), kind=kOutput, calls=%fused_computation.18 | convolution fusion | flops 3221225472 | bytes 29753344 | tf_op jit(solution)/shard_map/dot_general | solution.py:261
  16.8 0.5 convolution_bitcast_fusion.1
  17.3 0.0 copy-done.1
  17.3 0.5 fusion.1
  17.8 0.3 copy.29
  18.1 0.0 copy-done.3
  18.1 0.6 convolution_bitcast_fusion.2
  18.7 0.0 copy-start.2
  18.7 0.2 convolution_bitcast_fusion
  18.9 0.8 copy.22
  19.7 0.4 copy.24
  20.1 1.6 %reshape.27.half_ref = bf16[16,80,128]{2,1,0:T(8,128)(2,1)} reshape(bf16[128,8,160]{2,1,0:T(8,128)(2,1)S(1)} %copy.24) | data formatting | bytes 655360 | tf_op jit(solution)/shard_map/reshape | solution.py:250
  21.7 63.9 %shard_map.76 = (f32[160,1024]{1,0:T(8,128)}, f32[2,128,160]{2,1,0:T(8,128)}, bf16[16,80,128]{2,1,0:T(8,128)(2,1)}) custom-call(bf16[160,768]{1,0:T(8,128)(2,1)} %copy.25.cross_ref, bf16[768,16384]{1,0:T(8,128)(2,1)} %bitcast.39, f32[16,16,160]{2,1,0:T(8,128)} %bitcast.43, bf16[16,80,128]{2,1,0:T(8,128)(2,1)} %reshape.27.half_ref), custom_call_target="tpu_custom_call" | custom-call | flops 4026531840 | bytes 25165824 | tf_op jit(solution)/shard_map/pallas_call | solution.py:209
  85.6 3.7 %fusion.6 = f32[1024,128]{1,0:T(8,128)} fusion(f32[160,1024]{1,0:T(8,128)} %get-tuple-element.6, f32[2,128,160]{2,1,0:T(8,128)} %get-tuple-element.7), kind=kOutput, calls=%fused_computation.12 | convolution fusion | flops 251658240 | bytes 1310720 | tf_op jit(solution)/shard_map/ag,ra->gr/dot_general | solution.py:276
  89.4 1.5 %reshape_reshape.3 = bf16[128,8,160]{2,1,0:T(8,128)(2,1)S(1)} reshape(bf16[16,80,128]{2,1,0:T(8,128)(2,1)} %get-tuple-element.8) | data formatting | bytes 655360 | tf_op jit(solution)/shard_map/reshape;reshape | solution.py:275
  90.9 2.3 %fusion.4 = f32[128,8,128]{2,1,0:T(8,128)} fusion(bf16[128,8,160]{2,1,0:T(8,128)(2,1)S(1)} %reshape_reshape.3, f32[2,128,160]{2,1,0:T(8,128)} %get-tuple-element.7), kind=kOutput, calls=%fused_computation.10 | convolution fusion | flops 251658240 | bytes 983040 | tf_op jit(solution)/shard_map/rts,qs->rtq/dot_general | solution.py:277
  93.2 0.0 copy-done.2
  (1 shorter events, 0.0 us)
Async XLA Ops:
  0.6 1.1 %copy-start = (bf16[160,8,160]{2,1,0:T(8,128)(2,1)S(1)}, bf16[160,8,160]{2,1,0:T(8,128)(2,1)}, u32[]{:S(2)}) copy-start(bf16[160,8,160]{2,1,0:T(8,128)(2,1)} %param.8) | copy-start | bytes 1228804
  0.6 16.7 %copy-start.1 = (bf16[160,96]{1,0:T(8,128)(2,1)S(1)}, bf16[160,96]{1,0:T(8,128)(2,1)}, u32[]{:S(2)}) copy-start(bf16[160,96]{1,0:T(8,128)(2,1)} %param.9) | copy-start | bytes 92164
  0.7 17.4 %copy-start.3 = (bf16[128,8,128]{2,1,0:T(8,128)(2,1)S(1)}, bf16[128,8,128]{2,1,0:T(8,128)(2,1)}, u32[]{:S(2)}) copy-start(bf16[128,8,128]{2,1,0:T(8,128)(2,1)} %param.7) | copy-start | bytes 786436
  18.7 74.5 %copy-start.2 = (f32[96,128]{1,0:T(8,128)}, f32[96,128]{1,0:T(8,128)S(1)}, u32[]{:S(2)}) copy-start(f32[96,128]{1,0:T(8,128)S(1)} %convolution_bitcast_fusion.2) | copy-start | bytes 147460

commit v3 on v2

--- a/solution.py
+++ b/solution.py
@@ -58,8 +58,8 @@
 def sketch_kernel(
     n, rows, cross_ref, field_ref, wide_ref, half_ref, psi_ref, factor_out, half_out,
     chunk, a_send, a_recv, a_keep, b_send, b_recv, b_keep, c_send, c_recv,
-    w_recv, h_recv, w_all, h_all, omega_ref,
-    load_sem, a_ss, a_rs, b_ss, b_rs, c_ss, c_rs, w_ss, w_rs, h_ss, h_rs, w2_ss, w2_rs, h2_ss, h2_rs,
+    w_a, w_ak, w_b, w_bk, w_c, w_all, h_a, h_ak, h_b, h_bk, h_c, h_all,
+    load_sem, a_ss, a_rs, b_ss, b_rs, c_ss, c_rs, w_ss, w_rs, h_ss, h_rs,
 ):
     far = n // 4
     me = lax.axis_index("col")
@@ -85,24 +85,50 @@
 
     pl.semaphore_wait(barrier, n - 1)
 
-    def spread_wide(j):
-        to = lax.rem(me + j, n)
-        return remote(wide_ref.at[to], w_recv.at[j], w_ss.at[j], w_rs.at[j], to)
-
-    def spread_half(j):
-        to = lax.rem(me + j, n)
-        return remote(half_ref.at[to], h_recv.at[j], h_ss.at[j], h_rs.at[j], to)
-
-    def share_wide(j):
-        return remote(w_all.at[0], w_all.at[j], w2_ss.at[j], w2_rs.at[j], lax.rem(me + j, n))
-
-    def share_half(j):
-        return remote(h_all.at[0], h_all.at[j], h2_ss.at[j], h2_rs.at[j], lax.rem(me + j, n))
-
-    @pl.loop(1, n)
-    def _(j):
-        spread_wide(j).start()
-        spread_half(j).start()
+    small = (
+        (wide_ref, w_a, w_ak, w_b, w_bk, w_c, w_all, w_ss, w_rs),
+        (half_ref, h_a, h_ak, h_b, h_bk, h_c, h_all, h_ss, h_rs),
+    )
+    other_core, other_y = me + 1 - 2 * core, me + 2 - 4 * y
+
+    def small_copies(stage):
+        found = []
+        for source, a, ak, b, bk, c, whole, ss, rs in small:
+            mine = whole.at[z, y, core]
+            if stage == 0:
+                parts = [(source.at[:, :, 1 - core], a, 0, other_core)]
+            elif stage == 1:
+                parts = [(ak.at[:, 1 - y], b, 1, other_y)]
+            elif stage == 2:
+                parts = [(bk.at[goal(k)], c.at[k], 4 + k, (goal(k) * 2 + y) * 2 + core) for k in range(far - 1)]
+            elif stage == 3:
+                parts = [(mine, mine, 3 + far + k, (goal(k) * 2 + y) * 2 + core) for k in range(far - 1)]
+            elif stage == 4:
+                parts = [(whole.at[:, y, core], whole.at[:, y, core], 2, other_y)]
+            else:
+                parts = [(whole.at[:, :, core], whole.at[:, :, core], 3, other_core)]
+            found += [remote(src, dst, ss.at[i], rs.at[i], to) for src, dst, i, to in parts]
+        return found
+
+    def small_start(stage):
+        for copy in small_copies(stage):
+            copy.start()
+
+    def small_finish(stage):
+        for copy in small_copies(stage):
+            copy.wait()
+        for source, a, ak, b, bk, c, whole, _, _ in small:
+            if stage == 0:
+                ak[...] = (source[:, :, core].astype(jnp.float32) + a[...].astype(jnp.float32)).astype(ak.dtype)
+            elif stage == 1:
+                bk[...] = (ak[:, y].astype(jnp.float32) + b[...].astype(jnp.float32)).astype(bk.dtype)
+            elif stage == 2:
+                total = bk[z].astype(jnp.float32)
+                for k in range(far - 1):
+                    total += c[k].astype(jnp.float32)
+                whole[z, y, core] = total.astype(whole.dtype)
+
+    small_start(0)
 
     def copy_a(k):
         return remote(a_send.at[k], a_recv.at[k], a_ss.at[k], a_rs.at[k], me + 1 - 2 * core)
@@ -143,22 +169,10 @@
             psi_ref[...] = total
 
     def solve():
-        @pl.loop(1, n)
-        def _(j):
-            share_wide(j).wait()
-            share_half(j).wait()
-
-        omega_ref[me] = w_all[0]
-        half_out[me] = h_all[0]
-
-        @pl.loop(1, n)
-        def _(j):
-            source = lax.rem(me - j + n, n)
-            omega_ref[source] = w_all[j]
-            half_out[source] = h_all[j]
-
-        held = omega_ref.shape[1]
-        omega = omega_ref[...].reshape(n * held, omega_ref.shape[2])
+        small_finish(5)
+        half_out[...] = h_all[...]
+        held = w_all.shape[3]
+        omega = w_all[...].reshape(n * held, w_all.shape[4])
         if held != rows:
             to = lax.broadcasted_iota(jnp.int32, (n * rows, n * held), 0)
             at = lax.broadcasted_iota(jnp.int32, (n * rows, n * held), 1)
@@ -172,23 +186,10 @@
             compute(k)
         if 1 <= k <= far:
             stage_b(k - 1)
-        if k == min(1, far - 1):
-
-            @pl.loop(1, n)
-            def _(j):
-                spread_wide(j).wait()
-                spread_half(j).wait()
-
-            w_all[0] = lax.fori_loop(1, n, lambda j, s: s + w_recv[j], wide_ref[me])
-            h_all[0] = lax.fori_loop(
-                1, n, lambda j, s: s + h_recv[j].astype(jnp.float32), half_ref[me].astype(jnp.float32)
-            ).astype(jnp.bfloat16)
-
-            @pl.loop(1, n)
-            def _(j):
-                share_wide(j).start()
-                share_half(j).start()
-
+        stage = k - max(far - 4, 0)
+        if 0 <= stage < 5:
+            small_finish(stage)
+            small_start(stage + 1)
         if k == far + 1:
             solve()
         if k >= 2:
@@ -225,14 +226,14 @@
             pltpu.VMEM((far, rank, block), full),
             pltpu.VMEM((far, rank, block), low),
             pltpu.VMEM((far, rank, block), low),
-            pltpu.VMEM(wide.shape, full),
-            pltpu.VMEM(half.shape, low),
-            pltpu.VMEM(wide.shape, full),
-            pltpu.VMEM(half.shape, low),
-            pltpu.VMEM(wide.shape, full),
+            *[
+                pltpu.VMEM(lead + x.shape[3:], x.dtype)
+                for x in (wide, half)
+                for lead in ((far, 2), (far, 2), (far,), (far,), (far,), (far, 2, 2))
+            ],
             dma((2,)),
             *[dma((far,)) for _ in range(6)],
-            *[dma((n,)) for _ in range(8)],
+            *[dma((2 * far + 2,)) for _ in range(4)],
         ],
         compiler_params=pltpu.CompilerParams(
             collective_id=0, has_side_effects=True, vmem_limit_bytes=56 * 2**20
@@ -269,8 +270,11 @@
     rows = 2 * rank_left // n
     held = -(-rows // 8) * 8
     omega_term = jnp.pad(omega_term.reshape(n, rows, rank_right), ((0, 0), (0, held - rows), (0, 0)))
+    middle_rows = split_rows(middle_term.astype(jnp.bfloat16), n, 16)
     psi, factor, half = sketch(
-        n, rows, cross, flat, omega_term, split_rows(middle_term.astype(jnp.bfloat16), n, 16)
+        n, rows, cross, flat,
+        omega_term.reshape(n // 4, 2, 2, *omega_term.shape[1:]),
+        middle_rows.reshape(n // 4, 2, 2, *middle_rows.shape[1:]),
     )
     psi_middle = half.reshape(-1)[: middle_term.size].reshape(middle_term.shape).astype(jnp.float32)
     core_first = jnp.einsum("ag,ra->gr", psi, factor[0], precision=HIGH)

time: 93.7 us -> 85.6 us (0.914)
  Pallas kernels: 63.9 us -> 56 us
    pallas_call x1, Pallas kernels: 63.9 us -> 56 us  [sketch(): pl.pallas_call(functools.partial(sketch_kernel, n, rows), out_shape=(jax....]
    another operation x0 -> x1, local copies, waits for them, and re-layouts: none -> 1.58 us  [body(): middle_rows.reshape(n // 4, 2, 2, *middle_rows.shape[1:])]
    reshape x1 -> x0, local copies, waits for them, and re-layouts: 1.58 us -> none  [split_rows(): return x.reshape(n, rows, 128)]
where the time goes in v3:
time: 85.6 us; the launch traced here: 85.3 us
  Pallas kernels  56 us (65%)
  matrix products  21.6 us (25%)
  local copies, waits for them, and re-layouts  6.87 us (8%)
    pallas_call x1, Pallas kernels, sketch(): pl.pallas_call(functools.partial(sketch_kernel, n, rows), out_shape=(jax....  56 us
    dot_general x1, matrix products, body(): left = jnp.dot(flat, left_first, preferred_element_type=jnp.float32)  12.8 us
    dot_general x1, matrix products, body(): core_first = jnp.einsum('ag,ra->gr', psi, factor[0], precision=HIGH)  3.74 us
    dot_general x1, matrix products, body(): jnp.einsum('rts,qs->rtq', psi_middle, factor[1], precision=HIGH)  2.3 us

profile of v3, /device:TPU:13, one launch (start us, length us, event | category | flops | bytes accessed | tf_op | source)
XLA Modules:
  0.0 85.3 jit_solution(14326910788479604097)
XLA Ops:
  0.6 0.0 copy-start
  0.6 0.0 copy-start.1
  0.7 0.0 copy-start.3
  0.7 1.1 %copy-done = bf16[160,8,160]{2,1,0:T(8,128)(2,1)S(1)} copy-done((bf16[160,8,160]{2,1,0:T(8,128)(2,1)S(1)}, bf16[160,8,160]{2,1,0:T(8,128)(2,1)}, u32[]{:S(2)}) %copy-start) | copy-done | bytes 409624
  1.7 1.1 %fusion = bf16[160,96,8]{1,0,2:T(8,128)(2,1)S(1)} fusion(bf16[160,8,160]{2,1,0:T(8,128)(2,1)S(1)} %copy-done, bf16[160,96]{1,0:T(8,128)(2,1)} %param.9), kind=kOutput, calls=%fused_computation.2 | convolution fusion | flops 39444480 | bytes 686080 | tf_op jit(solution)/shard_map/atb,bc->act/dot_general | solution.py:259
  2.8 0.3 copy.19
  3.2 0.9 %copy.25.cross_ref = bf16[160,768]{1,0:T(8,128)(2,1)} copy(bf16[160,768]{0,1:T(8,128)(2,1)S(1)} %bitcast.44) | data formatting | bytes 491520 | tf_op jit(solution)/shard_map/reshape | solution.py:261
  4.0 12.8 %fusion.12 = f32[768,128]{1,0:T(8,128)S(1)} fusion(bf16[16384,128]{1,0:T(8,128)(2,1)} %param.6, bf16[96,8,16384]{2,1,0:T(8,128)(2,1)} %param.5), kind=kOutput, calls=%fused_computation.18 | convolution fusion | flops 3221225472 | bytes 29753344 | tf_op jit(solution)/shard_map/dot_general | solution.py:262
  16.8 0.5 convolution_bitcast_fusion.1
  17.3 0.0 copy-done.1
  17.3 0.5 fusion.1
  17.8 0.3 copy.29
  18.1 0.0 copy-done.3
  18.1 0.6 convolution_bitcast_fusion.2
  18.7 0.0 copy-start.2
  18.7 0.2 convolution_bitcast_fusion
  18.9 0.8 copy.22
  19.7 0.4 copy.24
  20.1 1.6 %reshape_reshape.6.half_ref = bf16[4,2,2,80,128]{4,3,2,1,0:T(8,128)(2,1)} reshape(bf16[128,8,160]{2,1,0:T(8,128)(2,1)S(1)} %copy.24) | data formatting | bytes 655360 | tf_op jit(solution)/shard_map/reshape;reshape | solution.py:277
  21.7 56.0 %shard_map.76 = (f32[160,1024]{1,0:T(8,128)}, f32[2,128,160]{2,1,0:T(8,128)}, bf16[4,2,2,80,128]{4,3,2,1,0:T(8,128)(2,1)}) custom-call(bf16[160,768]{1,0:T(8,128)(2,1)} %copy.25.cross_ref, bf16[768,16384]{1,0:T(8,128)(2,1)} %bitcast.41, f32[4,2,2,16,160]{4,3,2,1,0:T(8,128)} %bitcast.45, bf16[4,2,2,80,128]{4,3,2,1,0:T(8,128)(2,1)} %reshape_reshape.6.half_ref), custom_call_target="tpu_custom_call" | custom-call | flops 4026531840 | bytes 25165824 | tf_op jit(solution)/shard_map/pallas_call | solution.py:210
  77.8 3.7 %fusion.6 = f32[1024,128]{1,0:T(8,128)} fusion(f32[160,1024]{1,0:T(8,128)} %get-tuple-element.6, f32[2,128,160]{2,1,0:T(8,128)} %get-tuple-element.7), kind=kOutput, calls=%fused_computation.12 | convolution fusion | flops 251658240 | bytes 1310720 | tf_op jit(solution)/shard_map/ag,ra->gr/dot_general | solution.py:280
  81.5 1.5 %reshape_reshape.7 = bf16[128,8,160]{2,1,0:T(8,128)(2,1)S(1)} reshape(bf16[4,2,2,80,128]{4,3,2,1,0:T(8,128)(2,1)} %get-tuple-element.8) | data formatting | bytes 655360 | tf_op jit(solution)/shard_map/reshape;reshape | solution.py:279
  83.0 2.3 %fusion.4 = f32[128,8,128]{2,1,0:T(8,128)} fusion(bf16[128,8,160]{2,1,0:T(8,128)(2,1)S(1)} %reshape_reshape.7, f32[2,128,160]{2,1,0:T(8,128)} %get-tuple-element.7), kind=kOutput, calls=%fused_computation.10 | convolution fusion | flops 251658240 | bytes 983040 | tf_op jit(solution)/shard_map/rts,qs->rtq/dot_general | solution.py:281
  85.3 0.0 copy-done.2
  (1 shorter events, 0.0 us)
Async XLA Ops:
  0.6 1.1 %copy-start = (bf16[160,8,160]{2,1,0:T(8,128)(2,1)S(1)}, bf16[160,8,160]{2,1,0:T(8,128)(2,1)}, u32[]{:S(2)}) copy-start(bf16[160,8,160]{2,1,0:T(8,128)(2,1)} %param.8) | copy-start | bytes 1228804
  0.6 16.7 %copy-start.1 = (bf16[160,96]{1,0:T(8,128)(2,1)S(1)}, bf16[160,96]{1,0:T(8,128)(2,1)}, u32[]{:S(2)}) copy-start(bf16[160,96]{1,0:T(8,128)(2,1)} %param.9) | copy-start | bytes 92164
  0.7 17.4 %copy-start.3 = (bf16[128,8,128]{2,1,0:T(8,128)(2,1)S(1)}, bf16[128,8,128]{2,1,0:T(8,128)(2,1)}, u32[]{:S(2)}) copy-start(bf16[128,8,128]{2,1,0:T(8,128)(2,1)} %param.7) | copy-start | bytes 786436
  18.7 66.7 %copy-start.2 = (f32[96,128]{1,0:T(8,128)}, f32[96,128]{1,0:T(8,128)S(1)}, u32[]{:S(2)}) copy-start(f32[96,128]{1,0:T(8,128)S(1)} %convolution_bitcast_fusion.2) | copy-start | bytes 147460
